TPU v7x, 32 devices: a whole 2x2x4 slice. The times are simulated.
32 devices in a mesh: segment: 4 (over z), dp: 4 (over y, x), expert: 2 (over core).
Axes of the slice: x: 2, y: 2, z: 4, core: 2. Of those that a mesh axis runs over, the one named last changes fastest.
Arguments:
- fwd_inputs: bfloat16 [4, 512, 2048], P('segment', ('dp', 'expert')), may hold values from -17 to 17
- fwd_routes: int32 [4, 512, 8], P('segment', ('dp', 'expert')), may hold values from 0 to 15, as said below
- fwd_weights: float32 [4, 512, 8], P('segment', ('dp', 'expert')), may hold values from 0.2 to 0.6
- bwd_inputs: bfloat16 [4, 512, 2048], P('segment', ('dp', 'expert')), may hold values from -17 to 17
- bwd_cotangent: bfloat16 [4, 512, 2048], P('segment', ('dp', 'expert')), may hold values from -6 to 6
- bwd_routes: int32 [4, 512, 8], P('segment', ('dp', 'expert')), may hold values from 0 to 15, as said below
- bwd_weights: float32 [4, 512, 8], P('segment', ('dp', 'expert')), may hold values from 0.2 to 0.6
- norm_gain: float32 [4, 2048], P('segment'), may hold values from 0.5 to 2
- w_gate: bfloat16 [4, 16, 2048, 384], P('segment', ('dp', 'expert')), may hold values from -0.125 to 0.125
- w_up: bfloat16 [4, 16, 2048, 384], P('segment', ('dp', 'expert')), may hold values from -0.125 to 0.125
- w_down: bfloat16 [4, 16, 384, 2048], P('segment', ('dp', 'expert')), may hold values from -0.3125 to 0.3125
Outputs:
- next_forward: bfloat16 [4, 512, 2048], P('segment', ('dp', 'expert'))
- prev_grad: bfloat16 [4, 512, 2048], P('segment', ('dp', 'expert'))
Inputs may be any that keep to these rules, and one draw needn't show every extreme that they name: `fwd_routes`: each row names 8 different experts. Among the rows of one device no expert is named more than 36 times, and in each section one expert is named exactly 36 times on every device of that section. `bwd_routes`: each row names 8 different experts. Among the rows of one device no expert is named more than 36 times, and in each section one expert is named exactly 36 times on every device of that section.
All inputs are finite; a program needn't handle non-finite values.
Results may differ from a plain program's by a relative error of at most 0.0059.
Values may be sent and summed in bfloat16 or wider, within the bound.
A program may use at most 128 MiB of HBM per device.

v0:
```python
import jax
import jax.numpy as jnp
from jax import lax
from jax.sharding import PartitionSpec as P

EPSILON = 1e-06


def from_behind(value, axis, steps):
    count = lax.axis_size(axis)
    pairs = [(source, (source + steps) % count) for source in range(count)]
    return lax.ppermute(value, axis, pairs)


def normalize(inputs, norm_scale):
    values = inputs.astype(jnp.float32)
    inv_rms = lax.rsqrt(jnp.mean(values * values, axis=-1, keepdims=True) + EPSILON)
    return ((values * inv_rms * norm_scale).astype(jnp.bfloat16), values, inv_rms)


def slot_of(routes, experts_total, capacity):
    flat_routes = routes.reshape(-1)
    onehot = (flat_routes[:, None] == jnp.arange(experts_total, dtype=jnp.int32)[None, :]).astype(
        jnp.int32
    )
    before = jnp.cumsum(onehot, axis=0) - onehot
    position = jnp.sum(before * onehot, axis=1)
    return flat_routes * capacity + position


def pack(rows, slots, slot_total, top_count):
    row_count = rows.shape[0]
    source = jnp.arange(slots.shape[0], dtype=jnp.int32) // top_count
    owners = jnp.full((slot_total,), row_count, jnp.int32).at[slots].set(source)
    padded = jnp.concatenate([rows, jnp.zeros((1, rows.shape[1]), rows.dtype)], axis=0)
    return padded[owners]


def expert_work(fwd_rows, back_rows, cotangent_rows, gate_mat, up_mat, down_mat):
    gate_proj = jnp.einsum("gecd,edf->gecf", fwd_rows, gate_mat, preferred_element_type=jnp.float32)
    up_proj = jnp.einsum("gecd,edf->gecf", fwd_rows, up_mat, preferred_element_type=jnp.float32)
    activated = (gate_proj * jax.nn.sigmoid(gate_proj) * up_proj).astype(jnp.bfloat16)
    out_rows = jnp.einsum(
        "gecf,efd->gecd", activated, down_mat, preferred_element_type=jnp.float32
    ).astype(jnp.bfloat16)
    gate_back = jnp.einsum(
        "gecd,edf->gecf", back_rows, gate_mat, preferred_element_type=jnp.float32
    )
    up_back = jnp.einsum("gecd,edf->gecf", back_rows, up_mat, preferred_element_type=jnp.float32)
    back_hidden = jnp.einsum(
        "gecd,efd->gecf", cotangent_rows, down_mat, preferred_element_type=jnp.float32
    )
    sigmoid_gate = jax.nn.sigmoid(gate_back)
    d_gate = (
        back_hidden * up_back * sigmoid_gate * (1.0 + gate_back * (1.0 - sigmoid_gate))
    ).astype(jnp.bfloat16)
    d_up = (back_hidden * gate_back * sigmoid_gate).astype(jnp.bfloat16)
    d_normed = (
        jnp.einsum("gecf,edf->gecd", d_gate, gate_mat, preferred_element_type=jnp.float32)
        + jnp.einsum("gecf,edf->gecd", d_up, up_mat, preferred_element_type=jnp.float32)
    ).astype(jnp.bfloat16)
    return (out_rows, d_normed)


def body(
    fwd_inputs,
    fwd_routes,
    fwd_weights,
    bwd_inputs,
    bwd_cotangent,
    bwd_routes,
    bwd_weights,
    norm_gain,
    w_gate,
    w_up,
    w_down,
):
    inputs = fwd_inputs[0]
    tokens = inputs.shape[0]
    model_width = inputs.shape[1]
    top_count = fwd_routes.shape[2]
    groups_dp = lax.axis_size("dp")
    groups_expert = lax.axis_size("expert")
    group_size = groups_dp * groups_expert
    local_experts = w_gate.shape[1]
    experts_total = local_experts * group_size
    capacity = (9 * tokens * top_count + 8 * experts_total - 1) // (8 * experts_total)
    slot_total = experts_total * capacity
    norm_scale = norm_gain[0]
    normed_fwd = normalize(inputs, norm_scale)[0]
    normed_bwd, back_values, back_rms = normalize(bwd_inputs[0], norm_scale)
    fwd_slots = slot_of(fwd_routes[0], experts_total, capacity)
    bwd_slots = slot_of(bwd_routes[0], experts_total, capacity)
    packed_fwd = pack(normed_fwd, fwd_slots, slot_total, top_count)
    packed_bwd = pack(normed_bwd, bwd_slots, slot_total, top_count)
    packed_cot = pack(bwd_cotangent[0], bwd_slots, slot_total, top_count)
    arrived = (
        lax.all_to_all(packed_fwd, ("dp", "expert"), split_axis=0, concat_axis=0, tiled=True),
        lax.all_to_all(packed_bwd, ("dp", "expert"), split_axis=0, concat_axis=0, tiled=True),
        lax.all_to_all(packed_cot, ("dp", "expert"), split_axis=0, concat_axis=0, tiled=True),
    )
    block_shape = (group_size, local_experts, capacity, model_width)
    out_rows, d_rows = expert_work(
        arrived[0].reshape(block_shape),
        arrived[1].reshape(block_shape),
        arrived[2].reshape(block_shape),
        w_gate[0],
        w_up[0],
        w_down[0],
    )
    returned = (
        lax.all_to_all(
            out_rows.reshape(slot_total, model_width),
            ("dp", "expert"),
            split_axis=0,
            concat_axis=0,
            tiled=True,
        ),
        lax.all_to_all(
            d_rows.reshape(slot_total, model_width),
            ("dp", "expert"),
            split_axis=0,
            concat_axis=0,
            tiled=True,
        ),
    )
    fwd_back = returned[0][fwd_slots].reshape(tokens, top_count, model_width)
    bwd_back = returned[1][bwd_slots].reshape(tokens, top_count, model_width)
    combined = jnp.sum(fwd_back.astype(jnp.float32) * fwd_weights[0][:, :, None], axis=1)
    section_out = (inputs.astype(jnp.float32) + combined).astype(jnp.bfloat16)
    norm_grad = jnp.sum(bwd_back.astype(jnp.float32) * bwd_weights[0][:, :, None], axis=1)
    scaled = norm_scale * norm_grad
    section_grad = (
        bwd_cotangent[0].astype(jnp.float32)
        + back_rms * scaled
        - back_values * back_rms**3 * jnp.mean(back_values * scaled, axis=-1, keepdims=True)
    ).astype(jnp.bfloat16)
    next_forward = from_behind(section_out[None], "segment", 1)
    prev_grad = from_behind(section_grad[None], "segment", -1)
    return (next_forward, prev_grad)


def solution(mesh):
    placed = (
        P("segment", ("dp", "expert"), None),
        P("segment", ("dp", "expert"), None),
        P("segment", ("dp", "expert"), None),
        P("segment", ("dp", "expert"), None),
        P("segment", ("dp", "expert"), None),
        P("segment", ("dp", "expert"), None),
        P("segment", ("dp", "expert"), None),
        P("segment", None),
        P("segment", ("dp", "expert"), None, None),
        P("segment", ("dp", "expert"), None, None),
        P("segment", ("dp", "expert"), None, None),
    )
    return jax.shard_map(
        body,
        mesh=mesh,
        in_specs=placed,
        out_specs=(P("segment", ("dp", "expert"), None), P("segment", ("dp", "expert"), None)),
        check_vma=False,
    )
```

profile of v0, /device:TPU:0, one launch (start us, length us, event | category | flops | bytes accessed | tf_op | source)
XLA Modules:
  0.0 244.6 jit_solution(16982105897886666137)
XLA Ops:
  4.2 2.4 scatter_custom_fusion.1
  8.9 4.0 %gather_fusion.3 = bf16[576,2048]{1,0:T(8,128)(2,1)} fusion(bf16[65,2048]{1,0:T(8,128)(2,1)S(1)} %concatenate.11, s32[1024]{0:T(1024)S(1)} %pad_clamp_fusion.1), kind=kCustom, calls=%fused_computation.3 | custom fusion | bytes 4720896 | tf_op jit(solution)/shard_map/gather | solution.py:36
  12.8 5.2 %all-to-all-start.3 = ((bf16[8,72,2048]{2,1,0:T(8,128)(2,1)}), bf16[8,72,2048]{2,1,0:T(8,128)(2,1)}, u32[]{:S(2)}, u32[]{:S(2)}) async-start(bf16[8,72,2048]{2,1,0:T(8,128)(2,1)} %bitcast.194), calls=%async_computation.3 | async-start | bytes 4718592 | tf_op jit(solution)/shard_map/all_to_all | solution.py:99
  19.0 4.0 %gather_fusion.2 = bf16[576,2048]{1,0:T(8,128)(2,1)} fusion(bf16[65,2048]{1,0:T(8,128)(2,1)S(1)} %concatenate.10, s32[1024]{0:T(1024)S(1)} %pad_clamp_fusion.1), kind=kCustom, calls=%fused_computation.2 | custom fusion | bytes 4720896 | tf_op jit(solution)/shard_map/gather | solution.py:36
  23.0 24.6 %all-to-all-done.3 = bf16[8,72,2048]{2,1,0:T(8,128)(2,1)} async-done(((bf16[8,72,2048]{2,1,0:T(8,128)(2,1)}), bf16[8,72,2048]{2,1,0:T(8,128)(2,1)}, u32[]{:S(2)}, u32[]{:S(2)}) %all-to-all-start.3) | async-done | bytes 2359328 | tf_op jit(solution)/shard_map/all_to_all | solution.py:99
  47.6 4.9 %all-to-all-start.2 = ((bf16[8,72,2048]{2,1,0:T(8,128)(2,1)}), bf16[8,72,2048]{2,1,0:T(8,128)(2,1)}, u32[]{:S(2)}, u32[]{:S(2)}) async-start(bf16[8,72,2048]{2,1,0:T(8,128)(2,1)} %bitcast.193), calls=%async_computation.2 | async-start | bytes 4718592 | tf_op jit(solution)/shard_map/all_to_all | solution.py:100
  52.5 3.0 %copy.49 = bf16[8,72,2048]{2,0,1:T(8,128)(2,1)S(1)} copy(bf16[8,72,2048]{2,1,0:T(8,128)(2,1)} %all-to-all-done.3) | data formatting | bytes 4718592 | tf_op jit(solution)/shard_map/all_to_all | solution.py:99
  59.2 22.2 %all-to-all-done.2 = bf16[8,72,2048]{2,1,0:T(8,128)(2,1)} async-done(((bf16[8,72,2048]{2,1,0:T(8,128)(2,1)}), bf16[8,72,2048]{2,1,0:T(8,128)(2,1)}, u32[]{:S(2)}, u32[]{:S(2)}) %all-to-all-start.2) | async-done | bytes 2359328 | tf_op jit(solution)/shard_map/all_to_all | solution.py:100
  81.4 3.1 %copy.48 = bf16[8,72,2048]{2,0,1:T(8,128)(2,1)S(1)} copy(bf16[8,72,2048]{2,1,0:T(8,128)(2,1)} %all-to-all-done.2) | data formatting | bytes 4718592 | tf_op jit(solution)/shard_map/all_to_all | solution.py:100
  93.2 2.9 %copy.53 = bf16[8,72,2048]{2,1,0:T(8,128)(2,1)} copy(bf16[8,72,2048]{2,0,1:T(8,128)(2,1)S(1)} %bitcast.191) | data formatting | bytes 4718592 | tf_op jit(solution)/shard_map/all_to_all | solution.py:119
  96.0 4.5 %all-to-all-start.4 = ((bf16[8,72,2048]{2,1,0:T(8,128)(2,1)}), bf16[8,72,2048]{2,1,0:T(8,128)(2,1)}, u32[]{:S(2)}, u32[]{:S(2)}) async-start(bf16[8,72,2048]{2,1,0:T(8,128)(2,1)} %copy.53), calls=%async_computation.4 | async-start | bytes 4718592 | tf_op jit(solution)/shard_map/all_to_all | solution.py:119
  102.6 2.4 scatter_custom_fusion
  105.3 24.7 %all-to-all-done.4 = bf16[8,72,2048]{2,1,0:T(8,128)(2,1)} async-done(((bf16[8,72,2048]{2,1,0:T(8,128)(2,1)}), bf16[8,72,2048]{2,1,0:T(8,128)(2,1)}, u32[]{:S(2)}, u32[]{:S(2)}) %all-to-all-start.4) | async-done | bytes 2359328 | tf_op jit(solution)/shard_map/all_to_all | solution.py:119
  130.0 7.2 %gather_fusion.4 = bf16[512,2048]{1,0:T(8,128)(2,1)} fusion(bf16[576,2048]{1,0:T(8,128)(2,1)} %bitcast.41, s32[1024]{0:T(1024)S(1)} %pad_clamp_fusion), kind=kCustom, calls=%fused_computation.4 | custom fusion | bytes 4196352 | tf_op jit(solution)/shard_map/gather | solution.py:128
  137.2 3.5 %fusion = f32[64,2048]{1,0:T(8,128)S(1)} fusion(bf16[512,2048]{1,0:T(8,128)(2,1)} %gather_fusion.4, f32[64,8]{1,0:T(8,128)S(1)} %copy.54), kind=kLoop, calls=%fused_computation.9 | loop fusion | flops 3014656 | bytes 2623488 | tf_op jit(solution)/shard_map/reduce_sum | solution.py:131
  141.6 4.0 %gather_fusion = bf16[576,2048]{1,0:T(8,128)(2,1)} fusion(bf16[65,2048]{1,0:T(8,128)(2,1)S(1)} %concatenate.9, s32[1024]{0:T(1024)S(1)} %pad_clamp_fusion.3), kind=kCustom, calls=%fused_computation | custom fusion | bytes 4720896 | tf_op jit(solution)/shard_map/gather | solution.py:36
  145.6 33.1 %all_to_all.51 = bf16[8,72,2048]{2,1,0:T(8,128)(2,1)S(1)} all-to-all(bf16[8,72,2048]{2,1,0:T(8,128)(2,1)} %bitcast.195), channel_id=1, replica_groups=mesh['segment'=4,'dp'=4,'expert'=2] {'dp','expert'}, dimensions={0} | all-to-all | bytes 4718592 | tf_op jit(solution)/shard_map/all_to_all | solution.py:98
  186.7 2.7 %copy.42 = bf16[8,72,2048]{2,1,0:T(8,128)(2,1)} copy(bf16[8,72,2048]{2,0,1:T(8,128)(2,1)S(1)} %bitcast.192) | data formatting | bytes 4718592 | tf_op jit(solution)/shard_map/all_to_all | solution.py:112
  189.4 4.5 %all-to-all-start.1 = ((bf16[8,72,2048]{2,1,0:T(8,128)(2,1)}), bf16[8,72,2048]{2,1,0:T(8,128)(2,1)}, u32[]{:S(2)}, u32[]{:S(2)}) async-start(bf16[8,72,2048]{2,1,0:T(8,128)(2,1)} %copy.42), calls=%async_computation.1 | async-start | bytes 4718592 | tf_op jit(solution)/shard_map/all_to_all | solution.py:112
  196.1 4.2 %collective-permute-start.1 = (bf16[1,64,2048]{2,1,0:T(8,128)(2,1)}, bf16[1,64,2048]{2,1,0:T(8,128)(2,1)S(1)}, u32[]{:S(2)}, u32[]{:S(2)}) collective-permute-start(bf16[1,64,2048]{2,1,0:T(8,128)(2,1)} %fusion.70), channel_id=1, source_target_pairs={{0,24},{8,0},{16,8},{24,16},{1,25},{9,1},{17,9},{25,17},{2,26},{10... | collective-permute-start | bytes 786440 | tf_op jit(solution)/shard_map/ppermute | solution.py:12
  200.3 23.1 %all-to-all-done.1 = bf16[8,72,2048]{2,1,0:T(8,128)(2,1)} async-done(((bf16[8,72,2048]{2,1,0:T(8,128)(2,1)}), bf16[8,72,2048]{2,1,0:T(8,128)(2,1)}, u32[]{:S(2)}, u32[]{:S(2)}) %all-to-all-start.1) | async-done | bytes 2359328 | tf_op jit(solution)/shard_map/all_to_all | solution.py:112
  223.3 7.5 %gather_fusion.1 = bf16[512,2048]{1,0:T(8,128)(2,1)} fusion(bf16[576,2048]{1,0:T(8,128)(2,1)} %bitcast.20, s32[1024]{0:T(1024)S(1)} %pad_clamp_fusion.2), kind=kCustom, calls=%fused_computation.1 | custom fusion | bytes 4196352 | tf_op jit(solution)/shard_map/gather | solution.py:127
  230.8 3.5 %fusion.1 = f32[64,2048]{1,0:T(8,128)S(1)} fusion(bf16[512,2048]{1,0:T(8,128)(2,1)} %gather_fusion.1, f32[64,8]{1,0:T(8,128)S(1)} %copy.43), kind=kLoop, calls=%fused_computation.11 | loop fusion | flops 3014656 | bytes 2623488 | tf_op jit(solution)/shard_map/reduce_sum | solution.py:129
  236.5 6.4 %collective-permute-done = bf16[1,64,2048]{2,1,0:T(8,128)(2,1)S(1)} collective-permute-done((bf16[1,64,2048]{2,1,0:T(8,128)(2,1)S(1)}, bf16[1,64,2048]{2,1,0:T(8,128)(2,1)S(1)}, u32[]{:S(2)}, u32[]{:S(2)}) %collective-permute-start) | collective-permute-done | bytes 262176 | tf_op jit(solution)/shard_map/ppermute | solution.py:12
  (96 shorter events, 35.9 us)
Async XLA Ops:
  0.6 56.3 %copy-start = (bf16[1,2,2048,384]{3,2,1,0:T(8,128)(2,1)S(1)}, bf16[1,2,2048,384]{3,2,1,0:T(8,128)(2,1)}, u32[]{:S(2)}) copy-start(bf16[1,2,2048,384]{3,2,1,0:T(8,128)(2,1)} %param.19) | copy-start | bytes 9437188
  12.8 34.7 %all-to-all-start.3 = ((bf16[8,72,2048]{2,1,0:T(8,128)(2,1)}), bf16[8,72,2048]{2,1,0:T(8,128)(2,1)}, u32[]{:S(2)}, u32[]{:S(2)}) async-start(bf16[8,72,2048]{2,1,0:T(8,128)(2,1)} %bitcast.194), calls=%async_computation.3 | async-start | bytes 4718592 | tf_op jit(solution)/shard_map/all_to_all | solution.py:99
  47.6 33.8 %all-to-all-start.2 = ((bf16[8,72,2048]{2,1,0:T(8,128)(2,1)}), bf16[8,72,2048]{2,1,0:T(8,128)(2,1)}, u32[]{:S(2)}, u32[]{:S(2)}) async-start(bf16[8,72,2048]{2,1,0:T(8,128)(2,1)} %bitcast.193), calls=%async_computation.2 | async-start | bytes 4718592 | tf_op jit(solution)/shard_map/all_to_all | solution.py:100
  55.5 1.4 copy-start.1
  81.4 3.1 %copy-start.6 = (bf16[1,2,384,2048]{3,2,1,0:T(8,128)(2,1)S(1)}, bf16[1,2,384,2048]{3,2,1,0:T(8,128)(2,1)}, u32[]{:S(2)}) copy-start(bf16[1,2,384,2048]{3,2,1,0:T(8,128)(2,1)} %param.21) | copy-start | bytes 9437188
  81.4 3.1 %copy-start.12 = (f32[8,2,36,384]{3,0,2,1:T(8,128)S(1)}, f32[8,2,36,384]{3,0,2,1:T(8,128)}, u32[]{:S(2)}) copy-start(f32[8,2,36,384]{3,0,2,1:T(8,128)} %fusion.46) | copy-start | bytes 2654212
  84.6 1.7 copy-start.2
  84.6 2.6 %copy-start.8 = (bf16[1,2,2048,384]{3,2,1,0:T(8,128)(2,1)S(1)}, bf16[1,2,2048,384]{3,2,1,0:T(8,128)(2,1)}, u32[]{:S(2)}) copy-start(bf16[1,2,2048,384]{3,2,1,0:T(8,128)(2,1)} %param.20) | copy-start | bytes 9437188
  96.0 4.5 %copy-start.14 = (s32[1,64,8]{1,2,0:T(8,128)S(1)}, s32[1,64,8]{1,2,0:T(8,128)}, u32[]{:S(2)}) copy-start(s32[1,64,8]{1,2,0:T(8,128)} %param.12) | copy-start | bytes 6148
  96.0 4.8 %copy-start.15 = (f32[1,64,8]{1,2,0:T(8,128)S(1)}, f32[1,64,8]{1,2,0:T(8,128)}, u32[]{:S(2)}) copy-start(f32[1,64,8]{1,2,0:T(8,128)} %param.17) | copy-start | bytes 6148
  96.0 9.1 %copy-start.10 = (bf16[1,64,2048]{2,1,0:T(8,128)(2,1)S(1)}, bf16[1,64,2048]{2,1,0:T(8,128)(2,1)}, u32[]{:S(2)}) copy-start(bf16[1,64,2048]{2,1,0:T(8,128)(2,1)} %param.11) | copy-start | bytes 786436
  96.0 34.0 %all-to-all-start.4 = ((bf16[8,72,2048]{2,1,0:T(8,128)(2,1)}), bf16[8,72,2048]{2,1,0:T(8,128)(2,1)}, u32[]{:S(2)}, u32[]{:S(2)}) async-start(bf16[8,72,2048]{2,1,0:T(8,128)(2,1)} %copy.53), calls=%async_computation.4 | async-start | bytes 4718592 | tf_op jit(solution)/shard_map/all_to_all | solution.py:119
  137.2 3.5 %copy-start.4 = (bf16[1,64,2048]{2,1,0:T(8,128)(2,1)S(1)}, bf16[1,64,2048]{2,1,0:T(8,128)(2,1)}, u32[]{:S(2)}) copy-start(bf16[1,64,2048]{2,1,0:T(8,128)(2,1)} %param.14) | copy-start | bytes 786436
  137.2 3.5 %copy-start.13 = (f32[1,2048]{1,0:T(1,128)S(1)}, f32[1,2048]{1,0:T(1,128)}, u32[]{:S(2)}) copy-start(f32[1,2048]{1,0:T(1,128)} %param.18) | copy-start | bytes 24580
  140.7 0.8 copy-start.3
  180.0 1.9 copy-start.9
  181.9 1.9 copy-start.7
  189.4 4.5 %copy-start.16 = (f32[1,64,8]{1,2,0:T(8,128)S(1)}, f32[1,64,8]{1,2,0:T(8,128)}, u32[]{:S(2)}) copy-start(f32[1,64,8]{1,2,0:T(8,128)} %param.13) | copy-start | bytes 6148
  189.4 4.6 %copy-start.5 = (bf16[1,64,2048]{2,1,0:T(8,128)(2,1)S(1)}, bf16[1,64,2048]{2,1,0:T(8,128)(2,1)}, u32[]{:S(2)}) copy-start(bf16[1,64,2048]{2,1,0:T(8,128)(2,1)} %param.14) | copy-start | bytes 786436
  189.4 34.0 %all-to-all-start.1 = ((bf16[8,72,2048]{2,1,0:T(8,128)(2,1)}), bf16[8,72,2048]{2,1,0:T(8,128)(2,1)}, u32[]{:S(2)}, u32[]{:S(2)}) async-start(bf16[8,72,2048]{2,1,0:T(8,128)(2,1)} %copy.42), calls=%async_computation.1 | async-start | bytes 4718592 | tf_op jit(solution)/shard_map/all_to_all | solution.py:112
  196.1 40.5 %collective-permute-start.1 = (bf16[1,64,2048]{2,1,0:T(8,128)(2,1)}, bf16[1,64,2048]{2,1,0:T(8,128)(2,1)S(1)}, u32[]{:S(2)}, u32[]{:S(2)}) collective-permute-start(bf16[1,64,2048]{2,1,0:T(8,128)(2,1)} %fusion.70), channel_id=1, source_target_pairs={{0,24},{8,0},{16,8},{24,16},{1,25},{9,1},{17,9},{25,17},{2,26},{10... | collective-permute-start | bytes 786440 | tf_op jit(solution)/shard_map/ppermute | solution.py:12
  230.8 3.5 %copy-start.11 = (bf16[1,64,2048]{2,1,0:T(8,128)(2,1)S(1)}, bf16[1,64,2048]{2,1,0:T(8,128)(2,1)}, u32[]{:S(2)}) copy-start(bf16[1,64,2048]{2,1,0:T(8,128)(2,1)} %param.11) | copy-start | bytes 786436
  234.4 8.6 %collective-permute-start = (bf16[1,64,2048]{2,1,0:T(8,128)(2,1)S(1)}, bf16[1,64,2048]{2,1,0:T(8,128)(2,1)S(1)}, u32[]{:S(2)}, u32[]{:S(2)}) collective-permute-start(bf16[1,64,2048]{2,1,0:T(8,128)(2,1)S(1)} %fusion.63), channel_id=1, source_target_pairs={{0,8},{8,16},{16,24},{24,0},{1,9},{9,17},{17,25},{25,1},{2,10},{10... | collective-permute-start | bytes 786440 | tf_op jit(solution)/shard_map/ppermute | solution.py:12
where the time goes:
time: 249 us; the launch traced here: 245 us
  waiting for transfers between devices  101 us (41%)
  local copies, waits for them, and re-layouts  56 us (22%)
  blocking collectives  33.1 us (13%)
  starting transfers between devices  25.4 us (10%)
  other arithmetic  15 us (6%)
  matrix products  12.8 us (5%)
    all_to_all x1, blocking collectives, body(): lax.all_to_all(packed_fwd, ('dp', 'expert'), split_axis=0, concat_axis=0,...  33.1 us
    all_to_all x1, waiting for transfers between devices, body(): lax.all_to_all(d_rows.reshape(slot_total, model_width), ('dp', 'expert'),...  24.7 us
    all_to_all x1, waiting for transfers between devices, body(): lax.all_to_all(packed_bwd, ('dp', 'expert'), split_axis=0, concat_axis=0,...  24.6 us
    all_to_all x1, waiting for transfers between devices, body(): lax.all_to_all(out_rows.reshape(slot_total, model_width), ('dp', 'expert'...  23.1 us
    all_to_all x1, waiting for transfers between devices, body(): lax.all_to_all(packed_cot, ('dp', 'expert'), split_axis=0, concat_axis=0,...  22.2 us
    gather x3, local copies, waits for them, and re-layouts, pack(): return padded[owners]  12 us
    gather x1, local copies, waits for them, and re-layouts, body(): fwd_back = returned[0][fwd_slots].reshape(tokens, top_count, model_width)  7.48 us
    gather x1, local copies, waits for them, and re-layouts, body(): bwd_back = returned[1][bwd_slots].reshape(tokens, top_count, model_width)  7.22 us
  transfers between devices with their start and end apart: 6, of which 5 were waited for; matrix products, arithmetic and copies ran while one was open for 11% of the time, Pallas kernels for 0%

commit v1 on v0

v1 whole, which is shorter than its diff:
```python
import jax
import jax.numpy as jnp
from jax import lax
from jax.sharding import PartitionSpec as P

EPSILON = 1e-06
GROUP = ("dp", "expert")
BLOCKS = 8


def from_behind(value, axis, steps):
    count = lax.axis_size(axis)
    pairs = [(source, (source + steps) % count) for source in range(count)]
    return lax.ppermute(value, axis, pairs)


def normalize(inputs, norm_scale):
    values = inputs.astype(jnp.float32)
    inv_rms = lax.rsqrt(jnp.mean(values * values, axis=-1, keepdims=True) + EPSILON)
    return ((values * inv_rms * norm_scale).astype(jnp.bfloat16), values, inv_rms)


def dense_weights(routes, weights, experts_total):
    onehot = routes[:, :, None] == jnp.arange(experts_total, dtype=jnp.int32)
    return jnp.sum(jnp.where(onehot, weights[:, :, None], 0.0), axis=1)


def dot(a, b):
    return jnp.dot(a, b, preferred_element_type=jnp.float32)


def dot_t(a, b):
    return lax.dot_general(a, b, (((1,), (1,)), ((), ())), preferred_element_type=jnp.float32)


def by_blocks(work, block, *operands):
    count = operands[0].shape[0] // block
    if count == 1:
        return work(*operands)
    cut = [value.reshape(count, block, *value.shape[1:]) for value in operands]
    made = lax.map(lambda parts: work(*parts), tuple(cut))
    return made.reshape(count * block, made.shape[-1])


def body(
    fwd_inputs,
    fwd_routes,
    fwd_weights,
    bwd_inputs,
    bwd_cotangent,
    bwd_routes,
    bwd_weights,
    norm_gain,
    w_gate,
    w_up,
    w_down,
):
    local_experts = w_gate.shape[1]
    experts_total = local_experts * lax.axis_size("dp") * lax.axis_size("expert")
    first = local_experts * (lax.axis_index("dp") * lax.axis_size("expert") + lax.axis_index("expert"))
    norm_scale = norm_gain[0]
    both = jnp.stack(
        [
            dense_weights(fwd_routes[0], fwd_weights[0], experts_total),
            dense_weights(bwd_routes[0], bwd_weights[0], experts_total),
        ],
        axis=1,
    )
    both = lax.all_gather(both, GROUP, axis=0, tiled=True)
    both = lax.dynamic_slice_in_dim(both, first, local_experts, axis=2)
    normed_fwd = normalize(fwd_inputs[0], norm_scale)[0]
    normed_bwd, back_values, back_rms = normalize(bwd_inputs[0], norm_scale)
    fwd_rows = lax.all_gather(normed_fwd, GROUP, axis=0, tiled=True)
    bwd_rows = lax.all_gather(normed_bwd, GROUP, axis=0, tiled=True)
    cot_rows = lax.all_gather(bwd_cotangent[0], GROUP, axis=0, tiled=True)

    def forward(rows, factors):
        partial = 0.0
        for e in range(local_experts):
            gate = dot(rows, w_gate[0, e])
            up = dot(rows, w_up[0, e])
            act = gate * jax.nn.sigmoid(gate) * up * factors[:, e : e + 1]
            partial = partial + dot(act.astype(jnp.bfloat16), w_down[0, e])
        return partial.astype(jnp.bfloat16)

    def backward(rows, cotangents, factors):
        partial = 0.0
        for e in range(local_experts):
            gate = dot(rows, w_gate[0, e])
            up = dot(rows, w_up[0, e])
            hidden = dot_t(cotangents, w_down[0, e]) * factors[:, e : e + 1]
            q = jax.nn.sigmoid(gate)
            d_gate = (hidden * up * q * (1.0 + gate * (1.0 - q))).astype(jnp.bfloat16)
            d_up = (hidden * gate * q).astype(jnp.bfloat16)
            partial = partial + dot_t(d_gate, w_gate[0, e]) + dot_t(d_up, w_up[0, e])
        return partial.astype(jnp.bfloat16)

    block = BLOCKS * fwd_inputs.shape[1]
    partial = by_blocks(forward, block, fwd_rows, both[:, 0])
    combined = lax.psum_scatter(partial, GROUP, scatter_dimension=0, tiled=True)
    section_out = (fwd_inputs[0].astype(jnp.float32) + combined.astype(jnp.float32)).astype(jnp.bfloat16)
    next_forward = from_behind(section_out[None], "segment", 1)

    partial = by_blocks(backward, block, bwd_rows, cot_rows, both[:, 1])
    norm_grad = lax.psum_scatter(
        partial, GROUP, scatter_dimension=0, tiled=True
    ).astype(jnp.float32)
    scaled = norm_scale * norm_grad
    section_grad = (
        bwd_cotangent[0].astype(jnp.float32)
        + back_rms * scaled
        - back_values * back_rms**3 * jnp.mean(back_values * scaled, axis=-1, keepdims=True)
    ).astype(jnp.bfloat16)
    prev_grad = from_behind(section_grad[None], "segment", -1)
    return (next_forward, prev_grad)


def solution(mesh):
    rows = P("segment", GROUP, None)
    wide = P("segment", GROUP, None, None)
    return jax.shard_map(
        body,
        mesh=mesh,
        in_specs=(rows,) * 7 + (P("segment", None),) + (wide,) * 3,
        out_specs=(rows, rows),
        check_vma=False,
    )
```

time: 249 us -> 260 us (1.044); the launches traced: 245 us -> 260 us
  waiting for transfers between devices: 101 us -> 154 us
  local copies, waits for them, and re-layouts: 56 us -> 6.65 us
  matrix products: 12.8 us -> 59.3 us
  blocking collectives: 33.1 us -> 11.3 us
  starting transfers between devices: 25.4 us -> 5.25 us
  between operations: 1.28 us -> 13.9 us
  other arithmetic: 15 us -> 9.88 us
    all_to_all x4 -> x0, waiting for transfers between devices: 94.6 us -> none  [the longest x1 24.7 us: body(): lax.all_to_all(d_rows.reshape(slot_total, model_width), ('dp', 'expert'),...]
    reduce_scatter x0 -> x2, waiting for transfers between devices: none -> 77.2 us  [the longest x1 40 us: body(): lax.psum_scatter(partial, GROUP, scatter_dimension=0, tiled=True)]
    all_gather x0 -> x3, waiting for transfers between devices: none -> 67.4 us  [the longest x1 26.7 us: body(): fwd_rows = lax.all_gather(normed_fwd, GROUP, axis=0, tiled=True)]
    dot_general x8 -> x12, matrix products: 12.8 us -> 59.3 us  [the longest x6 32.6 us: dot_t(): lax.dot_general(a, b, (((1,), (1,)), ((), ())), preferred_element_type=jn...]
    all_to_all x1 -> x0, blocking collectives: 33.1 us -> none  [body(): lax.all_to_all(packed_fwd, ('dp', 'expert'), split_axis=0, concat_axis=0,...]
    gather x5 -> x0, local copies, waits for them, and re-layouts: 26.7 us -> none  [the longest x3 12 us: pack(): return padded[owners]]
    all_to_all x4 -> x0, starting transfers between devices: 19.1 us -> none  [the longest x1 5.17 us: body(): lax.all_to_all(packed_bwd, ('dp', 'expert'), split_axis=0, concat_axis=0,...]
    all_to_all x5 -> x0, local copies, waits for them, and re-layouts: 12.9 us -> none  [the longest x1 3.11 us: body(): lax.all_to_all(packed_cot, ('dp', 'expert'), split_axis=0, concat_axis=0,...]
  transfers between devices with their start and end apart: 6 -> 7, of which waited for: 5 -> 6; matrix products, arithmetic and copies ran while one was open for 11% -> 4% of each run, Pallas kernels for 0% -> 0%
where the time goes in v1:
time: 260 us
  waiting for transfers between devices  154 us (59%)
  matrix products  59.3 us (23%)
  between operations  13.9 us (5%)
  blocking collectives  11.3 us (4%)
  other arithmetic  9.88 us (4%)
  local copies, waits for them, and re-layouts  6.65 us (3%)
  starting transfers between devices  5.25 us (2%)
    reduce_scatter x1, waiting for transfers between devices, body(): lax.psum_scatter(partial, GROUP, scatter_dimension=0, tiled=True)  40 us
    reduce_scatter x1, waiting for transfers between devices, body(): combined = lax.psum_scatter(partial, GROUP, scatter_dimension=0, tiled=True)  37.1 us
    dot_general x6, matrix products, dot_t(): lax.dot_general(a, b, (((1,), (1,)), ((), ())), preferred_element_type=jn...  32.6 us
    dot_general x6, matrix products, dot(): return jnp.dot(a, b, preferred_element_type=jnp.float32)  26.7 us
    all_gather x1, waiting for transfers between devices, body(): fwd_rows = lax.all_gather(normed_fwd, GROUP, axis=0, tiled=True)  26.7 us
    all_gather x1, waiting for transfers between devices, body(): cot_rows = lax.all_gather(bwd_cotangent[0], GROUP, axis=0, tiled=True)  25.7 us
    all_gather x1, waiting for transfers between devices, body(): bwd_rows = lax.all_gather(normed_bwd, GROUP, axis=0, tiled=True)  15.1 us
    all_gather x1, blocking collectives, body(): both = lax.all_gather(both, GROUP, axis=0, tiled=True)  11.3 us
  transfers between devices with their start and end apart: 7, of which 6 were waited for; matrix products, arithmetic and copies ran while one was open for 4% of the time, Pallas kernels for 0%

profile of v1, /device:TPU:0, one launch (start us, length us, event | category | flops | bytes accessed | tf_op | source)
XLA Modules:
  0.0 260.0 jit_solution(14938633449784186675)
XLA Ops:
  8.3 1.8 fusion.128
  12.5 11.3 %all_gather.13 = f32[512,2,16]{2,1,0:T(2,128)S(1)} all-gather(f32[64,2,16]{2,1,0:T(2,128)S(1)} %copy.30), channel_id=1, replica_groups=mesh['segment'=4,'dp'=4,'expert'=2] {'dp','expert'}, dimensions={0}, use_global_device_ids=true | all-gather | bytes 73728 | tf_op jit(solution)/shard_map/all_gather | solution.py:69
  23.8 1.8 constant_dynamic-slice_fusion.1
  26.0 15.1 %all-gather.7.cloned.1.call-done = bf16[512,2048]{1,0:T(8,128)(2,1)} async-done(((bf16[64,2048]{1,0:T(8,128)(2,1)}), bf16[512,2048]{1,0:T(8,128)(2,1)}) %all-gather.7.cloned.1.call-update) | async-done | bytes 2097168 | tf_op jit(solution)/shard_map/all_gather | solution.py:74
  41.1 4.2 %fusion.28 = f32[512,384]{1,0:T(8,128)} fusion(bf16[512,2048]{1,0:T(8,128)(2,1)} %all-gather.7.cloned.1.call-done, bf16[1,2,2048,384]{3,2,1,0:T(8,128)(2,1)} %param.19), kind=kOutput, calls=%fused_computation.30 | convolution fusion | flops 805306368 | bytes 4456448 | tf_op jit(solution)/shard_map/dot_general | solution.py:29
  45.2 25.7 %all-gather.9.cloned.1.call-done = bf16[1,512,2048]{2,1,0:T(8,128)(2,1)} async-done(((bf16[1,64,2048]{2,1,0:T(8,128)(2,1)}), bf16[1,512,2048]{2,1,0:T(8,128)(2,1)}) %all-gather.9.cloned.1.call-update) | async-done | bytes 2097168 | tf_op jit(solution)/shard_map/all_gather | solution.py:75
  70.9 3.5 %fusion.66 = f32[512,384]{1,0:T(8,128)S(1)} fusion(bf16[1,2,384,2048]{3,2,1,0:T(8,128)(2,1)} %param.21, bf16[1,512,2048]{2,1,0:T(8,128)(2,1)} %all-gather.9.cloned.1.call-done, f32[512]{0:T(512)S(1)} %get-tuple-element.2), kind=kOutput, calls=%fused_computation.48 | convolution fusion | flops 805502976 | bytes 4458496 | tf_op jit(solution)/shard_map/dot_general | solution.py:33
  74.4 3.3 %fusion.20 = f32[512,2048]{1,0:T(8,128)} fusion(bf16[1,2,2048,384]{3,2,1,0:T(8,128)(2,1)S(1)} %copy-done.1, f32[512,384]{1,0:T(8,128)S(1)} %fusion.66, f32[512,384]{1,0:T(8,128)S(1)} %copy-done.3), kind=kOutput, calls=%fused_computation.22 | convolution fusion | flops 806486016 | bytes 7340032 | tf_op jit(solution)/shard_map/dot_general | solution.py:33
  78.5 2.2 fusion.13
  80.6 6.9 %fusion.26 = f32[512,2048]{1,0:T(8,128)} fusion(bf16[1,2,2048,384]{3,2,1,0:T(8,128)(2,1)} %param.19, f32[512,384]{1,0:T(8,128)} %copy-done.4, bf16[512,2048]{1,0:T(8,128)(2,1)} %all-gather.7.cloned.1.call-done, bf16[1,2,2048,384]{3,2,1,0:T(8,128)(2,1)S(1)} %copy-done.1, f32[512,384]{1,0:T(8,128)} %fusion.28), kind=kOutput, calls=%fused_computation.28 | convolution fusion | flops 1612578816 | bytes 11010048 | tf_op jit(solution)/shard_map/dot_general | solution.py:33
  87.5 4.2 %fusion.71 = f32[512,384]{1,0:T(8,128)} fusion(bf16[1,2,384,2048]{3,2,1,0:T(8,128)(2,1)} %param.21, bf16[1,512,2048]{2,1,0:T(8,128)(2,1)} %all-gather.9.cloned.1.call-done, f32[512]{0:T(512)S(1)} %get-tuple-element.3), kind=kOutput, calls=%fused_computation.49 | convolution fusion | flops 805502976 | bytes 4458496 | tf_op jit(solution)/shard_map/dot_general | solution.py:33
  91.7 6.9 %fusion.11 = f32[512,2048]{1,0:T(8,128)} fusion(bf16[1,2,2048,384]{3,2,1,0:T(8,128)(2,1)} %param.19, f32[512,384]{1,0:T(8,128)} %fusion.71, bf16[512,2048]{1,0:T(8,128)(2,1)} %all-gather.7.cloned.1.call-done, bf16[1,2,2048,384]{3,2,1,0:T(8,128)(2,1)S(1)} %copy-done.1, f32[512,384]{1,0:T(8,128)} %fusion.13), kind=kOutput, calls=%fused_computation.13 | convolution fusion | flops 1612578816 | bytes 11010048 | tf_op jit(solution)/shard_map/dot_general | solution.py:33
  98.6 7.8 %add_convert_fusion = bf16[512,2048]{1,0:T(8,128)(2,1)} fusion(f32[512,2048]{1,0:T(8,128)} %fusion.11, f32[512,2048]{1,0:T(8,128)} %fusion.26, f32[512,2048]{1,0:T(8,128)} %fusion.20, bf16[1,2,2048,384]{3,2,1,0:T(8,128)(2,1)S(1)} %copy-done.1, f32[512,384]{1,0:T(8,128)} %fusion.71, f32[512,384]{1,0:T(8,128)} %fusion.13), kind=kOutput, calls=%fused_computation | convolution fusion | flops 810680320 | bytes 17825792 | tf_op jit(solution)/shard_map/dot_general | solution.py:33
  107.8 40.0 %reduce-scatter.5.cloned.1.call-done = bf16[64,2048]{1,0:T(8,128)(2,1)} async-done(((bf16[512,2048]{1,0:T(8,128)(2,1)}), bf16[64,2048]{1,0:T(8,128)(2,1)}) %reduce-scatter.5.cloned.1.call-update) | async-done | bytes 262160 | tf_op jit(solution)/shard_map/reduce_scatter | solution.py:105
  149.0 2.3 fusion.141
  152.7 26.7 %all-gather.5.cloned.1.call-done = bf16[512,2048]{1,0:T(8,128)(2,1)} async-done(((bf16[64,2048]{1,0:T(8,128)(2,1)}), bf16[512,2048]{1,0:T(8,128)(2,1)}) %all-gather.5.cloned.1.call-update) | async-done | bytes 2097168 | tf_op jit(solution)/shard_map/all_gather | solution.py:73
  179.4 4.4 %fusion.15 = f32[512,384]{1,0:T(8,128)} fusion(bf16[512,2048]{1,0:T(8,128)(2,1)} %all-gather.5.cloned.1.call-done, bf16[1,2,2048,384]{3,2,1,0:T(8,128)(2,1)} %param.19), kind=kOutput, calls=%fused_computation.17 | convolution fusion | flops 805306368 | bytes 4456448 | tf_op jit(solution)/shard_map/dot_general | solution.py:29
  183.7 2.1 fusion.30
  185.9 6.6 %fusion.18 = f32[512,2048]{1,0:T(8,128)} fusion(bf16[1,2,384,2048]{3,2,1,0:T(8,128)(2,1)} %param.21, bf16[512,2048]{1,0:T(8,128)(2,1)} %all-gather.5.cloned.1.call-done, bf16[1,2,2048,384]{3,2,1,0:T(8,128)(2,1)S(1)} %copy-done.1, f32[512,384]{1,0:T(8,128)} %fusion.30, f32[512]{0:T(512)S(1)} %get-tuple-element.5), kind=kOutput, calls=%fused_computation.20 | convolution fusion | flops 1611988992 | bytes 10225664 | tf_op jit(solution)/shard_map/dot_general | solution.py:29
  192.5 7.3 %add_convert_fusion.1 = bf16[512,2048]{1,0:T(8,128)(2,1)} fusion(f32[512,2048]{1,0:T(8,128)} %fusion.18, bf16[1,2,384,2048]{3,2,1,0:T(8,128)(2,1)} %param.21, bf16[512,2048]{1,0:T(8,128)(2,1)} %all-gather.5.cloned.1.call-done, bf16[1,2,2048,384]{3,2,1,0:T(8,128)(2,1)S(1)} %copy-done.1, f32[512,384]{1,0:T(8,128)} %fusion.15, f32[512]{0:T(512)S(1)} %get-tuple-element.4), kind=kOutput, calls=%fused_computation.1 | convolution fusion | flops 1614086144 | bytes 12322816 | tf_op jit(solution)/shard_map/dot_general | solution.py:29
  200.7 3.3 %collective-permute-start.1 = (bf16[1,64,2048]{2,1,0:T(8,128)(2,1)S(1)}, bf16[1,64,2048]{2,1,0:T(8,128)(2,1)S(1)}, u32[]{:S(2)}, u32[]{:S(2)}) collective-permute-start(bf16[1,64,2048]{2,1,0:T(8,128)(2,1)S(1)} %copy-done.5), channel_id=1, source_target_pairs={{0,24},{8,0},{16,8},{24,16},{1,25},{9,1},{17,9},{25,17},{2,26},{10... | collective-permute-start | bytes 786440 | tf_op jit(solution)/shard_map/ppermute | solution.py:14
  204.0 37.1 %reduce-scatter.3.cloned.1.call-done = bf16[64,2048]{1,0:T(8,128)(2,1)} async-done(((bf16[512,2048]{1,0:T(8,128)(2,1)}), bf16[64,2048]{1,0:T(8,128)(2,1)}) %reduce-scatter.3.cloned.1.call-update) | async-done | bytes 262160 | tf_op jit(solution)/shard_map/reduce_scatter | solution.py:100
  242.1 1.5 collective-permute-start
  243.7 8.3 %collective-permute-done = bf16[1,64,2048]{2,1,0:T(8,128)(2,1)S(1)} collective-permute-done((bf16[1,64,2048]{2,1,0:T(8,128)(2,1)S(1)}, bf16[1,64,2048]{2,1,0:T(8,128)(2,1)S(1)}, u32[]{:S(2)}, u32[]{:S(2)}) %collective-permute-start) | collective-permute-done | bytes 262176 | tf_op jit(solution)/shard_map/ppermute | solution.py:14
  (48 shorter events, 11.8 us)
Async XLA Ops:
  7.2 33.9 %all-gather.7.cloned.1.call-start = ((), (), s32[]{:S(2)}) async-start(), calls=%async_computation.4 | async-start | bytes 2359296 | tf_op jit(solution)/shard_map/all_gather | solution.py:74
  10.1 60.8 %all-gather.9.cloned.1.call-start = ((), (), s32[]{:S(2)}) async-start(), calls=%async_computation.6 | async-start | bytes 2359296 | tf_op jit(solution)/shard_map/all_gather | solution.py:75
  10.9 137.0 %reduce-scatter.5.cloned.1.call-start = ((), (), s32[]{:S(2)}) async-start(), calls=%async_computation.5 | async-start | bytes 2359296 | tf_op jit(solution)/shard_map/reduce_scatter | solution.py:105
  70.9 3.5 %copy-start.1 = (bf16[1,2,2048,384]{3,2,1,0:T(8,128)(2,1)S(1)}, bf16[1,2,2048,384]{3,2,1,0:T(8,128)(2,1)}, u32[]{:S(2)}) copy-start(bf16[1,2,2048,384]{3,2,1,0:T(8,128)(2,1)} %param.20) | copy-start | bytes 9437188
  70.9 3.5 %copy-start.3 = (f32[512,384]{1,0:T(8,128)S(1)}, f32[512,384]{1,0:T(8,128)}, u32[]{:S(2)}) copy-start(f32[512,384]{1,0:T(8,128)} %fusion.28) | copy-start | bytes 2359300
  74.4 3.4 %copy-start.4 = (f32[512,384]{1,0:T(8,128)}, f32[512,384]{1,0:T(8,128)S(1)}, u32[]{:S(2)}) copy-start(f32[512,384]{1,0:T(8,128)S(1)} %fusion.66) | copy-start | bytes 2359300
  74.4 3.4 %copy-start.7 = (bf16[1,2,2048,384]{3,2,1,0:T(8,128)(2,1)S(1)}, bf16[1,2,2048,384]{3,2,1,0:T(8,128)(2,1)}, u32[]{:S(2)}) copy-start(bf16[1,2,2048,384]{3,2,1,0:T(8,128)(2,1)} %param.19) | copy-start | bytes 9437188
  74.4 4.1 %copy-start.9 = (bf16[512,2048]{1,0:T(8,128)(2,1)S(1)}, bf16[512,2048]{1,0:T(8,128)(2,1)}, u32[]{:S(2)}) copy-start(bf16[512,2048]{1,0:T(8,128)(2,1)} %all-gather.7.cloned.1.call-done) | copy-start | bytes 6291460
  106.4 41.4 %copy-start = (bf16[1,64,2048]{2,1,0:T(8,128)(2,1)S(1)}, bf16[1,64,2048]{2,1,0:T(8,128)(2,1)}, u32[]{:S(2)}) copy-start(bf16[1,64,2048]{2,1,0:T(8,128)(2,1)} %param.14) | copy-start | bytes 786436
  106.4 41.4 %copy-start.6 = (f32[1,2048]{1,0:T(1,128)S(1)}, f32[1,2048]{1,0:T(1,128)}, u32[]{:S(2)}) copy-start(f32[1,2048]{1,0:T(1,128)} %param.18) | copy-start | bytes 24580
  106.5 72.9 %all-gather.5.cloned.1.call-start = ((), (), s32[]{:S(2)}) async-start(), calls=%async_computation.2 | async-start | bytes 2359296 | tf_op jit(solution)/shard_map/all_gather | solution.py:73
  151.3 89.8 %reduce-scatter.3.cloned.1.call-start = ((), (), s32[]{:S(2)}) async-start(), calls=%async_computation.3 | async-start | bytes 2359296 | tf_op jit(solution)/shard_map/reduce_scatter | solution.py:100
  179.3 4.4 %copy-start.8 = (bf16[1,2,2048,384]{3,2,1,0:T(8,128)(2,1)S(1)}, bf16[1,2,2048,384]{3,2,1,0:T(8,128)(2,1)}, u32[]{:S(2)}) copy-start(bf16[1,2,2048,384]{3,2,1,0:T(8,128)(2,1)} %param.19) | copy-start | bytes 9437188
  179.3 4.4 %copy-start.10 = (bf16[512,2048]{1,0:T(8,128)(2,1)S(1)}, bf16[512,2048]{1,0:T(8,128)(2,1)}, u32[]{:S(2)}) copy-start(bf16[512,2048]{1,0:T(8,128)(2,1)} %all-gather.5.cloned.1.call-done) | copy-start | bytes 6291460
  199.7 0.9 copy-start.5
  199.7 41.4 %copy-start.2 = (bf16[1,64,2048]{2,1,0:T(8,128)(2,1)S(1)}, bf16[1,64,2048]{2,1,0:T(8,128)(2,1)}, u32[]{:S(2)}) copy-start(bf16[1,64,2048]{2,1,0:T(8,128)(2,1)} %param.11) | copy-start | bytes 786436
  200.7 43.0 %collective-permute-start.1 = (bf16[1,64,2048]{2,1,0:T(8,128)(2,1)S(1)}, bf16[1,64,2048]{2,1,0:T(8,128)(2,1)S(1)}, u32[]{:S(2)}, u32[]{:S(2)}) collective-permute-start(bf16[1,64,2048]{2,1,0:T(8,128)(2,1)S(1)} %copy-done.5), channel_id=1, source_target_pairs={{0,24},{8,0},{16,8},{24,16},{1,25},{9,1},{17,9},{25,17},{2,26},{10... | collective-permute-start | bytes 786440 | tf_op jit(solution)/shard_map/ppermute | solution.py:14
  242.1 9.9 %collective-permute-start = (bf16[1,64,2048]{2,1,0:T(8,128)(2,1)S(1)}, bf16[1,64,2048]{2,1,0:T(8,128)(2,1)S(1)}, u32[]{:S(2)}, u32[]{:S(2)}) collective-permute-start(bf16[1,64,2048]{2,1,0:T(8,128)(2,1)S(1)} %fusion.142), channel_id=1, source_target_pairs={{0,8},{8,16},{16,24},{24,0},{1,9},{9,17},{17,25},{25,1},{2,10},{10... | collective-permute-start | bytes 786440 | tf_op jit(solution)/shard_map/ppermute | solution.py:14
Sparse Core Ops, SparseCore 0:
  10.5 30.5 all-gather.6
  43.0 27.8 all-gather.8
  106.6 41.2 reduce-scatter.4
  151.4 27.8 all-gather.4
  199.9 41.2 reduce-scatter.2

commit v2 on v1

--- a/solution.py
+++ b/solution.py
@@ -1,6 +1,10 @@
+import functools
+
 import jax
 import jax.numpy as jnp
 from jax import lax
+from jax.experimental import pallas as pl
+from jax.experimental.pallas import tpu as pltpu
 from jax.sharding import PartitionSpec as P
 
 EPSILON = 1e-06
@@ -115,11 +119,273 @@
     return (next_forward, prev_grad)
 
 
+LANES = 128
+VMEM_BYTES = 52 * 2**20
+
+
+def remote(src, dst, send, recv, device):
+    return pltpu.make_async_remote_copy(
+        src_ref=src, dst_ref=dst, send_sem=send, recv_sem=recv,
+        device_id=device, device_id_type=pl.DeviceIdType.MESH,
+    )
+
+
+def kernel(
+    n_seg, n_dp, experts_total,
+    fwd_ref, froute_ref, fweight_ref, bwd_ref, cot_ref, broute_ref, bweight_ref, gain_ref,
+    gate_hbm, up_hbm, down_hbm, next_ref, prev_ref,
+    gate_w, up_w, down_w, rows, factors, part, mate, summed, landed, hidden, act_a, act_b, outs,
+    load_sem, fac_send, fac_recv, row_send, row_recv, mate_send, mate_recv,
+    psend, precv, qsend, qrecv, shift_send, shift_recv,
+):
+    seg, dp, ex = lax.axis_index("segment"), lax.axis_index("dp"), lax.axis_index("expert")
+    me = dp * 2 + ex
+    group = n_dp * 2
+    other = 1 - ex
+    tokens, width = cot_ref.shape
+    local, _, inner = gate_w.shape
+    ahead, behind = lax.rem(seg + 1, n_seg), lax.rem(seg + n_seg - 1, n_seg)
+
+    loads = [
+        pltpu.make_async_copy(src, dst, load_sem.at[i])
+        for i, (src, dst) in enumerate(((down_hbm, down_w), (gate_hbm, gate_w), (up_hbm, up_w)))
+    ]
+    for copy in loads:
+        copy.start()
+
+    def member(k):
+        p = lax.rem(me + k, group)
+        return (seg, p // 2, lax.rem(p, 2))
+
+    barrier = pltpu.get_barrier_semaphore()
+    for k in range(1, group):
+        pl.semaphore_signal(barrier, inc=1, device_id=member(k), device_id_type=pl.DeviceIdType.MESH)
+    for s in (ahead, behind):
+        pl.semaphore_signal(barrier, inc=1, device_id=(s, dp, ex), device_id_type=pl.DeviceIdType.MESH)
+    pl.semaphore_wait(barrier, group + 1)
+
+    def start_rows(t):
+        copies = []
+        own = rows.at[t, dp, ex]
+        for k in range(1, n_dp):
+            copies.append(remote(own, own, row_send.at[t, k], row_recv.at[t, k], (seg, lax.rem(dp + k, n_dp), ex)))
+        copies.append(remote(own, own, mate_send.at[t, 0], mate_recv.at[t, 0], (seg, dp, other)))
+        for copy in copies:
+            copy.start()
+        return copies
+
+    def finish_rows(t, copies):
+        passed = [copies[-1]]
+        for k in range(1, n_dp):
+            copies[k - 1].wait_recv()
+            slot = rows.at[t, lax.rem(dp + n_dp - k, n_dp), ex]
+            copy = remote(slot, slot, mate_send.at[t, k], mate_recv.at[t, k], (seg, dp, other))
+            copy.start()
+            passed.append(copy)
+        for copy in passed:
+            copy.wait_recv()
+        return copies[:-1] + passed
+
+    rows[0, dp, ex] = cot_ref[...]
+    cot_copies = start_rows(0)
+    rows[1, dp, ex] = normalize(bwd_ref[...], gain_ref[...])[0]
+    bwd_copies = start_rows(1)
+
+    lane = lax.broadcasted_iota(jnp.int32, (tokens, LANES), 1)
+    dense = jnp.zeros((tokens, LANES), jnp.float32)
+    for base, routes, weights in ((0, froute_ref, fweight_ref), (experts_total, broute_ref, bweight_ref)):
+        for k in range(routes.shape[1]):
+            hit = lane == routes[:, k : k + 1] + base
+            dense = dense + jnp.where(hit, weights[:, k : k + 1], 0.0)
+    factors[me] = dense
+    fac_copies = [
+        remote(factors.at[me], factors.at[me], fac_send.at[k], fac_recv.at[k], member(k)) for k in range(1, group)
+    ]
+    for copy in fac_copies:
+        copy.start()
+    rows[2, dp, ex] = normalize(fwd_ref[...], gain_ref[...])[0]
+    fwd_copies = start_rows(2)
+
+    pair = 2 * tokens
+
+    def column(d, base, e):
+        table = factors[pl.ds(d * 2, 2)].reshape(pair, LANES)
+        spot = lax.broadcasted_iota(jnp.int32, (pair, LANES), 1) == base + me * local + e
+        return jnp.sum(jnp.where(spot, table, 0.0), axis=1, keepdims=True)
+
+    def scatter(t, product):
+        mates, sent = [None] * n_dp, []
+
+        def pass_on(k):
+            q = lax.rem(dp + k, n_dp)
+            mates[k].wait_recv()
+            if k:
+                both = part[t, q, ex].astype(jnp.float32) + mate[t, q].astype(jnp.float32)
+                summed[t, k] = both.astype(jnp.bfloat16)
+                copy = remote(summed.at[t, k], landed.at[t, k], qsend.at[t, k], qrecv.at[t, k], (seg, q, ex))
+                copy.start()
+                sent.append(copy)
+
+        order = list(range(1, n_dp)) + [0]
+        for i, k in enumerate(order):
+            q = lax.rem(dp + k, n_dp)
+            product(q)
+            mates[k] = remote(
+                part.at[t, q, other], mate.at[t, q], psend.at[t, k], precv.at[t, k], (seg, dp, other)
+            )
+            mates[k].start()
+            if i:
+                pass_on(order[i - 1])
+        pass_on(order[-1])
+        return mates, sent
+
+    tile = 512 if width % 512 == 0 else LANES
+
+    def tiles(t, q, make):
+        def step(i, carry):
+            at = pl.ds(pl.multiple_of(i * tile, tile), tile)
+            made = make(q, at).astype(jnp.bfloat16)
+            part[t, q, :, :, at] = made.reshape(2, tokens, tile)
+            return carry
+
+        lax.fori_loop(0, width // tile, step, 0)
+
+    def each(work):
+        def step(i, carry):
+            work(i // local, lax.rem(i, local))
+            return carry
+
+        lax.fori_loop(0, n_dp * local, step, 0)
+
+    def cot_work(d, e):
+        hidden[d, e] = dot_t(rows[0, d].reshape(pair, width), down_w[e])
+
+    def bwd_work(d, e):
+        x = rows[1, d].reshape(pair, width)
+        gate, up = dot(x, gate_w[e]), dot(x, up_w[e])
+        back = hidden[d, e] * column(d, experts_total, e)
+        q = jax.nn.sigmoid(gate)
+        act_a[d, e] = (back * up * q * (1.0 + gate * (1.0 - q))).astype(jnp.bfloat16)
+        act_b[d, e] = (back * gate * q).astype(jnp.bfloat16)
+
+    def bwd_product(q):
+        def make(q, at):
+            total = 0.0
+            for e in range(local):
+                total = total + dot_t(act_a[q, e], gate_w[e, at, :]) + dot_t(act_b[q, e], up_w[e, at, :])
+            return total
+
+        tiles(0, q, make)
+
+    def fwd_work(d, e):
+        x = rows[2, d].reshape(pair, width)
+        gate, up = dot(x, gate_w[e]), dot(x, up_w[e])
+        act_a[d, e] = (gate * jax.nn.sigmoid(gate) * up * column(d, 0, e)).astype(jnp.bfloat16)
+
+    def fwd_product(q):
+        def make(q, at):
+            total = 0.0
+            for e in range(local):
+                total = total + dot(act_a[q, e], down_w[e, :, at])
+            return total
+
+        tiles(1, q, make)
+
+    def gathered(t, sent):
+        total = part[t, dp, ex].astype(jnp.float32) + mate[t, dp].astype(jnp.float32)
+        for copy in sent:
+            copy.wait_recv()
+        for k in range(1, n_dp):
+            total = total + landed[t, k].astype(jnp.float32)
+        return total
+
+    cot_copies = finish_rows(0, cot_copies)
+    loads[0].wait()
+    each(cot_work)
+    bwd_copies = finish_rows(1, bwd_copies)
+    for copy in fac_copies:
+        copy.wait_recv()
+    loads[1].wait()
+    loads[2].wait()
+    each(bwd_work)
+    bwd_mates, bwd_sent = scatter(0, bwd_product)
+
+    fwd_copies = finish_rows(2, fwd_copies)
+    each(fwd_work)
+    fwd_mates, fwd_sent = scatter(1, fwd_product)
+
+    scaled = gain_ref[...] * gathered(0, bwd_sent)
+    _, values, inv_rms = normalize(bwd_ref[...], gain_ref[...])
+    mean = jnp.mean(values * scaled, axis=-1, keepdims=True)
+    outs[0] = (cot_ref[...].astype(jnp.float32) + inv_rms * scaled - values * inv_rms**3 * mean).astype(jnp.bfloat16)
+    back = remote(outs.at[0], prev_ref, shift_send.at[0], shift_recv.at[0], (behind, dp, ex))
+    back.start()
+    outs[1] = (fwd_ref[...].astype(jnp.float32) + gathered(1, fwd_sent)).astype(jnp.bfloat16)
+    on = remote(outs.at[1], next_ref, shift_send.at[1], shift_recv.at[1], (ahead, dp, ex))
+    on.start()
+    for copy in cot_copies + bwd_copies + fwd_copies + fac_copies + bwd_mates + fwd_mates + bwd_sent + fwd_sent:
+        copy.wait_send()
+    back.wait()
+    on.wait()
+
+
+def fused(n_seg, n_dp, *operands):
+    flat = [value[0] for value in operands]
+    flat[7] = operands[7]
+    tokens, width = flat[0].shape
+    local, _, inner = flat[8].shape
+    wide, dma = jnp.bfloat16, pltpu.SemaphoreType.DMA
+    block = (tokens, width)
+    out = jax.ShapeDtypeStruct(block, wide)
+    vmem = pl.BlockSpec(memory_space=pltpu.VMEM)
+    group = 2 * n_dp
+    made = pl.pallas_call(
+        functools.partial(kernel, n_seg, n_dp, group * local),
+        out_shape=(out, out),
+        in_specs=[vmem] * 8 + [pl.BlockSpec(memory_space=pl.ANY)] * 3,
+        out_specs=(vmem, vmem),
+        scratch_shapes=[
+            pltpu.VMEM(flat[8].shape, wide),
+            pltpu.VMEM(flat[9].shape, wide),
+            pltpu.VMEM(flat[10].shape, wide),
+            pltpu.VMEM((3, n_dp, 2) + block, wide),
+            pltpu.VMEM((group, tokens, LANES), jnp.float32),
+            pltpu.VMEM((2, n_dp, 2) + block, wide),
+            pltpu.VMEM((2, n_dp) + block, wide),
+            pltpu.VMEM((2, n_dp) + block, wide),
+            pltpu.VMEM((2, n_dp) + block, wide),
+            pltpu.VMEM((n_dp, local, 2 * tokens, inner), jnp.float32),
+            pltpu.VMEM((n_dp, local, 2 * tokens, inner), wide),
+            pltpu.VMEM((n_dp, local, 2 * tokens, inner), wide),
+            pltpu.VMEM((2,) + block, wide),
+            dma((3,)), dma((group,)), dma((group,)),
+            dma((3, n_dp)), dma((3, n_dp)), dma((3, n_dp)), dma((3, n_dp)),
+            dma((2, n_dp)), dma((2, n_dp)), dma((2, n_dp)), dma((2, n_dp)),
+            dma((2,)), dma((2,)),
+        ],
+        compiler_params=pltpu.CompilerParams(
+            collective_id=0, has_side_effects=True, vmem_limit_bytes=VMEM_BYTES
+        ),
+    )(*flat)
+    return (made[0][None], made[1][None])
+
+
+def whole(n_seg, n_dp, n_expert, *operands):
+    tokens, width = operands[0].shape[1:]
+    local = operands[8].shape[1]
+    group = n_dp * n_expert
+    rows_bytes = group * tokens * width * 2
+    small = 9 * rows_bytes + 3 * operands[8].size * 2 <= VMEM_BYTES * 3 // 4
+    if n_expert == 2 and n_dp > 1 and n_seg > 1 and 2 * group * local <= LANES and small:
+        return fused(n_seg, n_dp, *operands)
+    return body(*operands)
+
+
 def solution(mesh):
     rows = P("segment", GROUP, None)
     wide = P("segment", GROUP, None, None)
     return jax.shard_map(
-        body,
+        functools.partial(whole, mesh.shape["segment"], mesh.shape["dp"], mesh.shape["expert"]),
         mesh=mesh,
         in_specs=(rows,) * 7 + (P("segment", None),) + (wide,) * 3,
         out_specs=(rows, rows),

time: 260 us -> 93.3 us (0.36)
  waiting for transfers between devices: 154 us -> 0 us
  Pallas kernels: 0 us -> 84.3 us
  matrix products: 59.3 us -> 0 us
  between operations: 13.9 us -> 0.64 us
  blocking collectives: 11.3 us -> 0 us
  other arithmetic: 9.88 us -> 0 us
  starting transfers between devices: 5.25 us -> 0 us
    pallas_call x0 -> x1, Pallas kernels: none -> 84.3 us  [fused(): pl.pallas_call(functools.partial(kernel, n_seg, n_dp, group * local), out...]
    reduce_scatter x2 -> x0, waiting for transfers between devices: 77.2 us -> none  [the longest x1 40 us: body(): lax.psum_scatter(partial, GROUP, scatter_dimension=0, tiled=True)]
    all_gather x3 -> x0, waiting for transfers between devices: 67.4 us -> none  [the longest x1 26.7 us: body(): fwd_rows = lax.all_gather(normed_fwd, GROUP, axis=0, tiled=True)]
    dot_general x12 -> x0, matrix products: 59.3 us -> none  [the longest x6 32.6 us: dot_t(): lax.dot_general(a, b, (((1,), (1,)), ((), ())), preferred_element_type=jn...]
    all_gather x1 -> x0, blocking collectives: 11.3 us -> none  [body(): both = lax.all_gather(both, GROUP, axis=0, tiled=True)]
    ppermute x2 -> x0, waiting for transfers between devices: 8.34 us -> none  [from_behind(): return lax.ppermute(value, axis, pairs)]
    unnamed x24 -> x14, local copies, waits for them, and re-layouts: 3.09 us -> 8.03 us
    ppermute x2 -> x0, starting transfers between devices: 4.86 us -> none  [from_behind(): return lax.ppermute(value, axis, pairs)]
  transfers between devices with their start and end apart: 7 -> 0, of which waited for: 6 -> 0; matrix products, arithmetic and copies ran while one was open for 4% -> 0% of each run, Pallas kernels for 0% -> 0%
where the time goes in v2:
time: 93.3 us; the launch traced here: 92.9 us
  Pallas kernels  84.3 us (90%)
  local copies, waits for them, and re-layouts  8.03 us (9%)
    pallas_call x1, Pallas kernels, fused(): pl.pallas_call(functools.partial(kernel, n_seg, n_dp, group * local), out...  84.3 us
    unnamed x14, local copies, waits for them, and re-layouts  8.03 us

profile of v2, /device:TPU:0, one launch (start us, length us, event | category | flops | bytes accessed | tf_op | source)
XLA Modules:
  0.0 92.9 jit_solution(4330539686005279673)
XLA Ops:
  0.6 0.8 copy.13
  1.4 0.8 copy.14
  2.2 0.8 copy.15
  2.9 0.8 copy.16
  3.7 0.0 copy-start
  3.7 0.9 %copy-done = bf16[1,64,2048]{2,1,0:T(8,128)(2,1)S(1)} copy-done((bf16[1,64,2048]{2,1,0:T(8,128)(2,1)S(1)}, bf16[1,64,2048]{2,1,0:T(8,128)(2,1)}, u32[]{:S(2)}) %copy-start) | copy-done | bytes 262168
  4.7 0.0 copy-start.1
  4.7 0.9 %copy-done.1 = bf16[1,64,2048]{2,1,0:T(8,128)(2,1)S(1)} copy-done((bf16[1,64,2048]{2,1,0:T(8,128)(2,1)S(1)}, bf16[1,64,2048]{2,1,0:T(8,128)(2,1)}, u32[]{:S(2)}) %copy-start.1) | copy-done | bytes 262168
  5.6 0.0 copy-start.2
  5.6 0.9 %copy-done.2 = bf16[1,64,2048]{2,1,0:T(8,128)(2,1)S(1)} copy-done((bf16[1,64,2048]{2,1,0:T(8,128)(2,1)S(1)}, bf16[1,64,2048]{2,1,0:T(8,128)(2,1)}, u32[]{:S(2)}) %copy-start.2) | copy-done | bytes 262168
  6.6 0.0 copy-start.3
  6.6 0.7 copy-done.3
  7.3 84.3 %shard_map.122 = (bf16[64,2048]{1,0:T(8,128)(2,1)S(1)}, bf16[64,2048]{1,0:T(8,128)(2,1)S(1)}) custom-call(bf16[64,2048]{1,0:T(8,128)(2,1)S(1)} %bitcast.12, s32[64,8]{1,0:T(8,128)S(1)} %bitcast.17, f32[64,8]{1,0:T(8,128)S(1)} %bitcast.18, bf16[64,2048]{1,0:T(8,128)(2,1)S(1)} %bitcast.13, bf16[64,2048]{1,0:T(8,128)(2,1)S(1)} %bitcast.14, ...), custom_call_target="tpu_custom_call" | custom-call | tf_op jit(solution)/shard_map/pallas_call | solution.py:342
  91.5 0.7 copy.19
  92.2 0.7 copy.20
Async XLA Ops:
  3.7 0.9 %copy-start = (bf16[1,64,2048]{2,1,0:T(8,128)(2,1)S(1)}, bf16[1,64,2048]{2,1,0:T(8,128)(2,1)}, u32[]{:S(2)}) copy-start(bf16[1,64,2048]{2,1,0:T(8,128)(2,1)} %param.11) | copy-start | bytes 786436
  4.7 0.9 %copy-start.1 = (bf16[1,64,2048]{2,1,0:T(8,128)(2,1)S(1)}, bf16[1,64,2048]{2,1,0:T(8,128)(2,1)}, u32[]{:S(2)}) copy-start(bf16[1,64,2048]{2,1,0:T(8,128)(2,1)} %param.14) | copy-start | bytes 786436
  5.6 0.9 %copy-start.2 = (bf16[1,64,2048]{2,1,0:T(8,128)(2,1)S(1)}, bf16[1,64,2048]{2,1,0:T(8,128)(2,1)}, u32[]{:S(2)}) copy-start(bf16[1,64,2048]{2,1,0:T(8,128)(2,1)} %param.15) | copy-start | bytes 786436
  6.6 0.7 copy-start.3

commit v3 on v2

--- a/solution.py
+++ b/solution.py
@@ -144,6 +144,8 @@
     other = 1 - ex
     tokens, width = cot_ref.shape
     local, _, inner = gate_w.shape
+    cut = 2 if tokens % 32 == 0 else 1
+    halves = [pl.ds(h * (tokens // cut), tokens // cut) for h in range(cut)]
     ahead, behind = lax.rem(seg + 1, n_seg), lax.rem(seg + n_seg - 1, n_seg)
 
     loads = [
@@ -222,9 +224,12 @@
             if k:
                 both = part[t, q, ex].astype(jnp.float32) + mate[t, q].astype(jnp.float32)
                 summed[t, k] = both.astype(jnp.bfloat16)
-                copy = remote(summed.at[t, k], landed.at[t, k], qsend.at[t, k], qrecv.at[t, k], (seg, q, ex))
-                copy.start()
-                sent.append(copy)
+                for h, at in enumerate(halves):
+                    copy = remote(
+                        summed.at[t, k, at], landed.at[t, k, at], qsend.at[t, k, h], qrecv.at[t, k, h], (seg, q, ex)
+                    )
+                    copy.start()
+                    sent.append(copy)
 
         order = list(range(1, n_dp)) + [0]
         for i, k in enumerate(order):
@@ -291,12 +296,13 @@
 
         tiles(1, q, make)
 
-    def gathered(t, sent):
-        total = part[t, dp, ex].astype(jnp.float32) + mate[t, dp].astype(jnp.float32)
-        for copy in sent:
+    def gathered(t, sent, h):
+        at = halves[h]
+        total = part[t, dp, ex, at].astype(jnp.float32) + mate[t, dp, at].astype(jnp.float32)
+        for copy in sent[h::cut]:
             copy.wait_recv()
         for k in range(1, n_dp):
-            total = total + landed[t, k].astype(jnp.float32)
+            total = total + landed[t, k, at].astype(jnp.float32)
         return total
 
     cot_copies = finish_rows(0, cot_copies)
@@ -314,19 +320,27 @@
     each(fwd_work)
     fwd_mates, fwd_sent = scatter(1, fwd_product)
 
-    scaled = gain_ref[...] * gathered(0, bwd_sent)
-    _, values, inv_rms = normalize(bwd_ref[...], gain_ref[...])
-    mean = jnp.mean(values * scaled, axis=-1, keepdims=True)
-    outs[0] = (cot_ref[...].astype(jnp.float32) + inv_rms * scaled - values * inv_rms**3 * mean).astype(jnp.bfloat16)
-    back = remote(outs.at[0], prev_ref, shift_send.at[0], shift_recv.at[0], (behind, dp, ex))
-    back.start()
-    outs[1] = (fwd_ref[...].astype(jnp.float32) + gathered(1, fwd_sent)).astype(jnp.bfloat16)
-    on = remote(outs.at[1], next_ref, shift_send.at[1], shift_recv.at[1], (ahead, dp, ex))
-    on.start()
+    shifts = []
+
+    def shift(t, h, target, device):
+        copy = remote(outs.at[t, halves[h]], target.at[halves[h]], shift_send.at[t, h], shift_recv.at[t, h], device)
+        copy.start()
+        shifts.append(copy)
+
+    for h, at in enumerate(halves):
+        scaled = gain_ref[...] * gathered(0, bwd_sent, h)
+        _, values, inv_rms = normalize(bwd_ref[at], gain_ref[...])
+        mean = jnp.mean(values * scaled, axis=-1, keepdims=True)
+        grad = cot_ref[at].astype(jnp.float32) + inv_rms * scaled - values * inv_rms**3 * mean
+        outs[0, at] = grad.astype(jnp.bfloat16)
+        shift(0, h, prev_ref, (behind, dp, ex))
+    for h, at in enumerate(halves):
+        outs[1, at] = (fwd_ref[at].astype(jnp.float32) + gathered(1, fwd_sent, h)).astype(jnp.bfloat16)
+        shift(1, h, next_ref, (ahead, dp, ex))
     for copy in cot_copies + bwd_copies + fwd_copies + fac_copies + bwd_mates + fwd_mates + bwd_sent + fwd_sent:
         copy.wait_send()
-    back.wait()
-    on.wait()
+    for copy in shifts:
+        copy.wait()
 
 
 def fused(n_seg, n_dp, *operands):
@@ -360,8 +374,8 @@
             pltpu.VMEM((2,) + block, wide),
             dma((3,)), dma((group,)), dma((group,)),
             dma((3, n_dp)), dma((3, n_dp)), dma((3, n_dp)), dma((3, n_dp)),
-            dma((2, n_dp)), dma((2, n_dp)), dma((2, n_dp)), dma((2, n_dp)),
-            dma((2,)), dma((2,)),
+            dma((2, n_dp)), dma((2, n_dp)), dma((2, n_dp, 2)), dma((2, n_dp, 2)),
+            dma((2, 2)), dma((2, 2)),
         ],
         compiler_params=pltpu.CompilerParams(
             collective_id=0, has_side_effects=True, vmem_limit_bytes=VMEM_BYTES

time: 93.3 us -> 90.6 us (0.971)
  Pallas kernels: 84.3 us -> 81.6 us
    pallas_call x1, Pallas kernels: 84.3 us -> 81.6 us  [fused(): pl.pallas_call(functools.partial(kernel, n_seg, n_dp, group * local), out...]
where the time goes in v3:
time: 90.6 us; the launch traced here: 90.2 us
  Pallas kernels  81.6 us (90%)
  local copies, waits for them, and re-layouts  8.03 us (9%)
    pallas_call x1, Pallas kernels, fused(): pl.pallas_call(functools.partial(kernel, n_seg, n_dp, group * local), out...  81.6 us
    unnamed x14, local copies, waits for them, and re-layouts  8.03 us

profile of v3, /device:TPU:0, one launch (start us, length us, event | category | flops | bytes accessed | tf_op | source)
XLA Modules:
  0.0 90.2 jit_solution(9082788826893042963)
XLA Ops:
  0.6 0.8 copy.13
  1.4 0.8 copy.14
  2.2 0.8 copy.15
  2.9 0.8 copy.16
  3.7 0.0 copy-start
  3.7 0.9 %copy-done = bf16[1,64,2048]{2,1,0:T(8,128)(2,1)S(1)} copy-done((bf16[1,64,2048]{2,1,0:T(8,128)(2,1)S(1)}, bf16[1,64,2048]{2,1,0:T(8,128)(2,1)}, u32[]{:S(2)}) %copy-start) | copy-done | bytes 262168
  4.7 0.0 copy-start.1
  4.7 0.9 %copy-done.1 = bf16[1,64,2048]{2,1,0:T(8,128)(2,1)S(1)} copy-done((bf16[1,64,2048]{2,1,0:T(8,128)(2,1)S(1)}, bf16[1,64,2048]{2,1,0:T(8,128)(2,1)}, u32[]{:S(2)}) %copy-start.1) | copy-done | bytes 262168
  5.6 0.0 copy-start.2
  5.6 0.9 %copy-done.2 = bf16[1,64,2048]{2,1,0:T(8,128)(2,1)S(1)} copy-done((bf16[1,64,2048]{2,1,0:T(8,128)(2,1)S(1)}, bf16[1,64,2048]{2,1,0:T(8,128)(2,1)}, u32[]{:S(2)}) %copy-start.2) | copy-done | bytes 262168
  6.6 0.0 copy-start.3
  6.6 0.7 copy-done.3
  7.3 81.6 %shard_map.122 = (bf16[64,2048]{1,0:T(8,128)(2,1)S(1)}, bf16[64,2048]{1,0:T(8,128)(2,1)S(1)}) custom-call(bf16[64,2048]{1,0:T(8,128)(2,1)S(1)} %bitcast.12, s32[64,8]{1,0:T(8,128)S(1)} %bitcast.17, f32[64,8]{1,0:T(8,128)S(1)} %bitcast.18, bf16[64,2048]{1,0:T(8,128)(2,1)S(1)} %bitcast.13, bf16[64,2048]{1,0:T(8,128)(2,1)S(1)} %bitcast.14, ...), custom_call_target="tpu_custom_call" | custom-call | tf_op jit(solution)/shard_map/pallas_call | solution.py:356
  88.8 0.7 copy.19
  89.5 0.7 copy.20
Async XLA Ops:
  3.7 0.9 %copy-start = (bf16[1,64,2048]{2,1,0:T(8,128)(2,1)S(1)}, bf16[1,64,2048]{2,1,0:T(8,128)(2,1)}, u32[]{:S(2)}) copy-start(bf16[1,64,2048]{2,1,0:T(8,128)(2,1)} %param.11) | copy-start | bytes 786436
  4.7 0.9 %copy-start.1 = (bf16[1,64,2048]{2,1,0:T(8,128)(2,1)S(1)}, bf16[1,64,2048]{2,1,0:T(8,128)(2,1)}, u32[]{:S(2)}) copy-start(bf16[1,64,2048]{2,1,0:T(8,128)(2,1)} %param.14) | copy-start | bytes 786436
  5.6 0.9 %copy-start.2 = (bf16[1,64,2048]{2,1,0:T(8,128)(2,1)S(1)}, bf16[1,64,2048]{2,1,0:T(8,128)(2,1)}, u32[]{:S(2)}) copy-start(bf16[1,64,2048]{2,1,0:T(8,128)(2,1)} %param.15) | copy-start | bytes 786436
  6.6 0.7 copy-start.3
